TPU v7x, 32 devices: a whole 2x2x4 slice. The times are simulated.
32 devices in a mesh: row: 8 (over y, x, core), col: 4 (over z).
Axes of the slice: x: 2, y: 2, z: 4, core: 2. Of those that a mesh axis runs over, the one named last changes fastest.
Arguments:
- a_tiles: bfloat16 [8, 4, 4, 27, 128, 128], P('row', 'col'), as said below
- pattern: int32 [8, 4, 4, 27], P('row', 'col'), may hold values from 0 to 1, as said below
- t_tiles: bfloat16 [8, 4, 4, 128, 128], P('row', 'col'), may hold values from -6 to 6
- colour: int32 [8, 4, 4], replicated, may hold values from 0 to 7, as said below
Outputs:
- prolongator: bfloat16 [8, 4, 4, 8, 128, 128], P('row', 'col')
- restriction_t: bfloat16 [8, 4, 4, 8, 128, 128], P('row', 'col')
Inputs may be any that keep to these rules, and one draw needn't show every extreme that they name: pattern[x, y, z, 13] is 1; pattern[x, y, z, o] is 0 where block (x, y - dy, z) or block (x + dx, y, z + dz) lies outside the grid. colour[x, y, z] = 4 p(x) + 2 q(y) + r(z) with p, q, r each 0 or 1. `a_tiles`: the diagonal of every tile with o = 13 is 3.4 or more.
All inputs are finite; a program needn't handle non-finite values.
Results may differ from a plain program's by a relative error of at most 0.0065.
Values may be sent and summed in bfloat16 or wider, within the bound.
A program may use at most 64 MiB of HBM per device.

v0:
```python
import functools

import jax
import jax.numpy as jnp
from jax import lax
from jax.experimental import pallas as pl
from jax.experimental.pallas import tpu as pltpu
from jax.sharding import PartitionSpec as P

SLOTS = 8
OMEGA = 2.0 / 3.0
BF = jnp.bfloat16
F32 = jnp.float32


def kernel(
    nx, ny, nz, blk,
    pattern, colour, a_hbm, t_own, pro_hbm, res_hbm,
    a_v, th, td, tt, sbuf, rbuf, own, obuf,
    a_sem, th_send, th_recv, p_send, p_recv, o_sem,
):
    x = lax.axis_index("row")
    y = lax.axis_index("col")
    has_dst = (x > 0, x < nx - 1, y > 0, y < ny - 1)
    has_src = (x < nx - 1, x > 0, y < ny - 1, y > 0)
    peers = ((x - 1, y), (x + 1, y), (x, y - 1), (x, y + 1))

    def a_copy(z):
        return pltpu.make_async_copy(a_hbm.at[0, 0, z], a_v.at[z], a_sem.at[z])

    for z in range(nz):
        a_copy(z).start()

    barrier = pltpu.get_barrier_semaphore()
    for d in range(4):
        @pl.when(has_dst[d])
        def _():
            pl.semaphore_signal(
                barrier, inc=1, device_id=peers[d], device_id_type=pl.DeviceIdType.MESH
            )
    count = sum(h.astype(jnp.int32) for h in has_dst)
    pl.semaphore_wait(barrier, count)

    def t_copy(d):
        return pltpu.make_async_remote_copy(
            src_ref=t_own.at[0, 0], dst_ref=th.at[d],
            send_sem=th_send.at[d], recv_sem=th_recv.at[d],
            device_id=peers[d], device_id_type=pl.DeviceIdType.MESH,
        )

    def p_copy(d, z):
        return pltpu.make_async_remote_copy(
            src_ref=sbuf.at[d, z], dst_ref=rbuf.at[d, z],
            send_sem=p_send.at[d, z], recv_sem=p_recv.at[d, z],
            device_id=peers[d], device_id_type=pl.DeviceIdType.MESH,
        )

    for d in (2, 3, 0, 1):
        @pl.when(has_dst[d])
        def _():
            t_copy(d).start()

    for d in range(4):
        @pl.when(jnp.logical_not(has_src[d]))
        def _():
            th[d] = jnp.zeros(th.shape[1:], BF)
            rbuf[d] = jnp.zeros(rbuf.shape[1:], BF)

    def bit(value, shift):
        return ((value >> shift) & 1).astype(F32)

    def p_of(i):
        return bit(colour[jnp.clip(i, 0, nx - 1), 0, 0], 2)

    def q_of(j):
        return bit(colour[0, jnp.clip(j, 0, ny - 1), 0], 1)

    def r_of(z):
        return bit(colour[0, 0, z], 0)

    def hits(value):
        return (1.0 - value, value)

    def times(tile, scalar):
        return tile * jnp.full(tile.shape, scalar, F32).astype(BF)

    def place(dst, which, high, source):
        zero = jnp.zeros((blk, 4 * blk), BF)
        dst[which, 0:blk, :] = zero
        dst[which, (nz + 1) * blk : (nz + 2) * blk, :] = zero

        def step(z, carry):
            tile = source(z)
            rows = pl.ds(pl.multiple_of((z + 1) * blk, blk), blk)
            r = r_of(z)
            for h in range(2):
                for l in range(2):
                    dst[which, rows, pl.ds((2 * h + l) * blk, blk)] = times(
                        tile, hits(high)[h] * hits(r)[l]
                    )
            return carry

        lax.fori_loop(0, nz, step, 0)

    place(td, 1, p_of(x), lambda z: t_own[0, 0, z])
    place(tt, 1, q_of(y), lambda z: t_own[0, 0, z])

    def mask_step(z, carry):
        a_copy(z).wait()
        for o in range(27):
            a_v[z, o] = times(a_v[z, o], pattern[0, 0, z, o].astype(F32))
        return carry

    lax.fori_loop(0, nz, mask_step, 0)

    for d, dst, which, high in (
        (0, td, 2, p_of(x + 1)),
        (1, td, 0, p_of(x - 1)),
        (2, tt, 2, q_of(y + 1)),
        (3, tt, 0, q_of(y - 1)),
    ):
        @pl.when(has_src[d])
        def _():
            t_copy(d).wait_recv()
        place(dst, which, high, lambda z, d=d: th[d, z])

    def direct(z, y_steps):
        rows = pl.ds(pl.multiple_of(z * blk, blk), 3 * blk)
        right = jnp.concatenate([td[i, rows, :] for i in range(3)], axis=0)
        left = jnp.concatenate(
            [
                jnp.concatenate(
                    [a_v[z, i * 9 + (dy + 1) * 3 + k] for i in range(3) for k in range(3)], axis=1
                )
                for dy in y_steps
            ],
            axis=0,
        )
        return jnp.dot(left, right, preferred_element_type=F32)

    def transposed(z, x_steps):
        rows = pl.ds(pl.multiple_of(z * blk, blk), 3 * blk)
        right = jnp.concatenate([tt[j, rows, :] for j in range(3)], axis=0)
        left = jnp.concatenate(
            [
                jnp.concatenate(
                    [
                        a_v[jnp.clip(z - 1 + e, 0, nz - 1), (dx + 1) * 9 + (2 - j) * 3 + 2 - e]
                        for dx in x_steps
                    ],
                    axis=1,
                )
                for j in range(3)
                for e in range(3)
            ],
            axis=0,
        )
        return lax.dot_general(
            left, right, (((0,), (0,)), ((), ())), preferred_element_type=F32
        )

    def edge_step(z, carry):
        part = direct(z, (1, -1)).astype(BF)
        sbuf[2, z] = part[:blk]
        sbuf[3, z] = part[blk:]
        for d in (2, 3):
            @pl.when(has_dst[d])
            def _():
                p_copy(d, z).start()
        part = transposed(z, (-1, 1)).astype(BF)
        sbuf[0, z] = part[:blk]
        sbuf[1, z] = part[blk:]
        for d in (0, 1):
            @pl.when(has_dst[d])
            def _():
                p_copy(d, z).start()
        return carry

    lax.fori_loop(0, nz, edge_step, 0)

    def own_step(z, carry):
        own[0, z] = direct(z, (0,))
        own[1, z] = transposed(z, (0,))
        return carry

    lax.fori_loop(0, nz, own_step, 0)

    px, qy = p_of(x), q_of(y)
    diagonal = lax.broadcasted_iota(jnp.int32, (blk, blk), 0) == lax.broadcasted_iota(
        jnp.int32, (blk, blk), 1
    )

    def out_copy(which, z):
        out = (pro_hbm, res_hbm)[which]
        return pltpu.make_async_copy(obuf.at[which, z], out.at[0, 0, z], o_sem.at[which, z])

    def final_step(z, carry):
        centre = jnp.where(diagonal, a_v[z, 13].astype(F32), 0.0)
        scale = OMEGA / jnp.sum(centre, axis=1, keepdims=True)
        tile = t_own[0, 0, z].astype(F32)
        r = r_of(z)
        for which in (1, 0):
            first = 2 if which == 0 else 0
            for d in (first, first + 1):
                @pl.when(has_src[d])
                def _():
                    p_copy(d, z).wait_recv()
            here, above, below = (
                (qy, q_of(y + 1), q_of(y - 1)) if which == 0 else (px, p_of(x + 1), p_of(x - 1))
            )
            for h in range(2):
                for l in range(2):
                    columns = pl.ds((2 * h + l) * blk, blk)
                    mine = own[which, z, :, columns] * scale
                    up = rbuf[first, z, :, columns].astype(F32) * scale
                    down = rbuf[first + 1, z, :, columns].astype(F32) * scale
                    for v in range(2):
                        total = (
                            mine * hits(here)[v] + up * hits(above)[v] + down * hits(below)[v]
                        )
                        p, q = (h, v) if which == 0 else (v, h)
                        keep = hits(px)[p] * hits(qy)[q] * hits(r)[l]
                        obuf[which, z, 4 * p + 2 * q + l] = (tile * keep - total).astype(BF)
            out_copy(which, z).start()
        return carry

    lax.fori_loop(0, nz, final_step, 0)

    for z in range(nz):
        out_copy(0, z).wait()
        out_copy(1, z).wait()
        for d in range(4):
            @pl.when(has_dst[d])
            def _():
                p_copy(d, z).wait_send()
    for d in range(4):
        @pl.when(has_dst[d])
        def _():
            t_copy(d).wait_send()


def body(nx, ny, a_tiles, pattern, t_tiles, colour):
    nz, blk = a_tiles.shape[2], a_tiles.shape[-1]
    out = jax.ShapeDtypeStruct((1, 1, nz, SLOTS, blk, blk), BF)
    return pl.pallas_call(
        functools.partial(kernel, nx, ny, nz, blk),
        out_shape=(out, out),
        in_specs=[
            pl.BlockSpec(memory_space=pltpu.SMEM),
            pl.BlockSpec(memory_space=pltpu.SMEM),
            pl.BlockSpec(memory_space=pl.ANY),
            pl.BlockSpec(memory_space=pltpu.VMEM),
        ],
        out_specs=(pl.BlockSpec(memory_space=pl.ANY),) * 2,
        scratch_shapes=[
            pltpu.VMEM((nz, 27, blk, blk), BF),
            pltpu.VMEM((4, nz, blk, blk), BF),
            pltpu.VMEM((3, (nz + 2) * blk, 4 * blk), BF),
            pltpu.VMEM((3, (nz + 2) * blk, 4 * blk), BF),
            pltpu.VMEM((4, nz, blk, 4 * blk), BF),
            pltpu.VMEM((4, nz, blk, 4 * blk), BF),
            pltpu.VMEM((2, nz, blk, 4 * blk), F32),
            pltpu.VMEM((2, nz, SLOTS, blk, blk), BF),
            pltpu.SemaphoreType.DMA((nz,)),
            pltpu.SemaphoreType.DMA((4,)),
            pltpu.SemaphoreType.DMA((4,)),
            pltpu.SemaphoreType.DMA((4, nz)),
            pltpu.SemaphoreType.DMA((4, nz)),
            pltpu.SemaphoreType.DMA((2, nz)),
        ],
        compiler_params=pltpu.CompilerParams(
            collective_id=0, has_side_effects=True, vmem_limit_bytes=48 * 1024 * 1024
        ),
        cost_estimate=pl.CostEstimate(
            flops=3_600_000_000, bytes_accessed=6_000_000, transcendentals=0
        ),
    )(pattern, colour, a_tiles, t_tiles)


def solution(mesh):
    in_specs = (
        P("row", "col", None, None, None, None),
        P("row", "col", None, None),
        P("row", "col", None, None, None),
        P(),
    )
    out_specs = (P("row", "col", None, None, None, None), P("row", "col", None, None, None, None))
    fn = functools.partial(body, mesh.shape["row"], mesh.shape["col"])
    return jax.shard_map(fn, mesh=mesh, in_specs=in_specs, out_specs=out_specs, check_vma=False)
```

profile of v0, /device:TPU:0, one launch (start us, length us, event | category | flops | bytes accessed | tf_op | source)
XLA Modules:
  0.0 32.2 jit_solution(1792777722707514855)
XLA Ops:
  0.6 0.8 %copy.6.colour = s32[8,4,4]{2,1,0:T(4,128)S(1)} copy(s32[8,4,4]{0,2,1:T(4,128)} %param.7) | data formatting | bytes 1024 | tf_op args[3]
  1.4 0.0 copy-start
  1.4 2.0 %copy-done = bf16[1,1,4,27,128,128]{5,4,3,2,1,0:T(8,128)(2,1)S(1)} copy-done((bf16[1,1,4,27,128,128]{5,4,3,2,1,0:T(8,128)(2,1)S(1)}, bf16[1,1,4,27,128,128]{5,4,3,2,1,0:T(8,128)(2,1)}, u32[]{:S(2)}) %copy-start) | copy-done | bytes 3538968
  3.4 0.0 copy-start.1
  3.4 0.9 %copy-done.1 = bf16[1,1,4,128,128]{4,3,2,1,0:T(8,128)(2,1)S(1)} copy-done((bf16[1,1,4,128,128]{4,3,2,1,0:T(8,128)(2,1)S(1)}, bf16[1,1,4,128,128]{4,3,2,1,0:T(8,128)(2,1)}, u32[]{:S(2)}) %copy-start.1) | copy-done | bytes 131096
  4.3 0.0 copy-start.2
  4.3 0.7 %copy-done.2 = s32[1,1,4,27]{3,2,1,0:T(4,128)S(1)} copy-done((s32[1,1,4,27]{3,2,1,0:T(4,128)S(1)}, s32[1,1,4,27]{3,2,1,0:T(4,128)}, u32[]{:S(2)}) %copy-start.2) | copy-done | bytes 456
  5.0 25.2 %shard_map.59 = (bf16[1,1,4,8,128,128]{5,4,3,2,1,0:T(8,128)(2,1)S(1)}, bf16[1,1,4,8,128,128]{5,4,3,2,1,0:T(8,128)(2,1)S(1)}) custom-call(s32[1,1,4,27]{3,2,1,0:T(4,128)S(1)} %copy-done.2, s32[8,4,4]{2,1,0:T(4,128)S(1)} %copy.6.colour, bf16[1,1,4,27,128,128]{5,4,3,2,1,0:T(8,128)(2,1)S(1)} %copy-done, bf16[1,1,4,128,128]{4,3,2,1,0:T(8,128)(2,1)S(1)} %copy-done.1), custom_call_target="tpu_custom_call" | custom-call | flops 3600000000 | bytes 6000000 | tf_op jit(solution)/shard_map/pallas_call | solution.py:245
  30.2 1.0 %copy.9 = bf16[1,1,4,8,128,128]{5,4,3,2,1,0:T(8,128)(2,1)} copy(bf16[1,1,4,8,128,128]{5,4,3,2,1,0:T(8,128)(2,1)S(1)} %get-tuple-element.4) | data formatting | bytes 2097152
  31.2 1.0 %copy.10 = bf16[1,1,4,8,128,128]{5,4,3,2,1,0:T(8,128)(2,1)} copy(bf16[1,1,4,8,128,128]{5,4,3,2,1,0:T(8,128)(2,1)S(1)} %get-tuple-element.5) | data formatting | bytes 2097152
Async XLA Ops:
  1.4 2.0 %copy-start = (bf16[1,1,4,27,128,128]{5,4,3,2,1,0:T(8,128)(2,1)S(1)}, bf16[1,1,4,27,128,128]{5,4,3,2,1,0:T(8,128)(2,1)}, u32[]{:S(2)}) copy-start(bf16[1,1,4,27,128,128]{5,4,3,2,1,0:T(8,128)(2,1)} %a_hbm.1) | copy-start | bytes 10616836
  3.4 0.9 %copy-start.1 = (bf16[1,1,4,128,128]{4,3,2,1,0:T(8,128)(2,1)S(1)}, bf16[1,1,4,128,128]{4,3,2,1,0:T(8,128)(2,1)}, u32[]{:S(2)}) copy-start(bf16[1,1,4,128,128]{4,3,2,1,0:T(8,128)(2,1)} %t_own.1) | copy-start | bytes 393220
  4.3 0.7 %copy-start.2 = (s32[1,1,4,27]{3,2,1,0:T(4,128)S(1)}, s32[1,1,4,27]{3,2,1,0:T(4,128)}, u32[]{:S(2)}) copy-start(s32[1,1,4,27]{3,2,1,0:T(4,128)} %pattern.1) | copy-start | bytes 1300
where the time goes:
time: 32.4 us; the launch traced here: 32.2 us
  Pallas kernels  25.2 us (78%)
  local copies, waits for them, and re-layouts  6.32 us (20%)
  between operations  0.64 us (2%)
    pallas_call x1, Pallas kernels, body(): pl.pallas_call(functools.partial(kernel, nx, ny, nz, blk), out_shape=(out...  25.2 us
    unnamed x9, local copies, waits for them, and re-layouts  6.32 us

commit v1 on v0

--- a/solution.py
+++ b/solution.py
@@ -15,9 +15,9 @@
 
 def kernel(
     nx, ny, nz, blk,
-    pattern, colour, a_hbm, t_own, pro_hbm, res_hbm,
-    a_v, th, td, tt, sbuf, rbuf, own, obuf,
-    a_sem, th_send, th_recv, p_send, p_recv, o_sem,
+    pattern_hbm, colour_hbm, a_hbm, t_hbm, pro, res,
+    pattern, colour, t_own, a_v, th, td, tt, sbuf, rbuf, own,
+    in_sem, a_sem, th_send, th_recv, p_send, p_recv,
 ):
     x = lax.axis_index("row")
     y = lax.axis_index("col")
@@ -28,6 +28,12 @@
     def a_copy(z):
         return pltpu.make_async_copy(a_hbm.at[0, 0, z], a_v.at[z], a_sem.at[z])
 
+    t_in = pltpu.make_async_copy(t_hbm, t_own, in_sem.at[0])
+    colour_in = pltpu.make_async_copy(colour_hbm, colour, in_sem.at[1])
+    pattern_in = pltpu.make_async_copy(pattern_hbm, pattern, in_sem.at[2])
+    colour_in.start()
+    pattern_in.start()
+    t_in.start()
     for z in range(nz):
         a_copy(z).start()
 
@@ -43,7 +49,7 @@
 
     def t_copy(d):
         return pltpu.make_async_remote_copy(
-            src_ref=t_own.at[0, 0], dst_ref=th.at[d],
+            src_ref=t_hbm.at[0, 0], dst_ref=th.at[d],
             send_sem=th_send.at[d], recv_sem=th_recv.at[d],
             device_id=peers[d], device_id_type=pl.DeviceIdType.MESH,
         )
@@ -70,13 +76,13 @@
         return ((value >> shift) & 1).astype(F32)
 
     def p_of(i):
-        return bit(colour[jnp.clip(i, 0, nx - 1), 0, 0], 2)
+        return bit(colour[0, 0, jnp.clip(i, 0, nx - 1)], 2)
 
     def q_of(j):
-        return bit(colour[0, jnp.clip(j, 0, ny - 1), 0], 1)
+        return bit(colour[jnp.clip(j, 0, ny - 1), 0, 0], 1)
 
     def r_of(z):
-        return bit(colour[0, 0, z], 0)
+        return bit(colour[0, z, 0], 0)
 
     def hits(value):
         return (1.0 - value, value)
@@ -102,8 +108,12 @@
 
         lax.fori_loop(0, nz, step, 0)
 
+    colour_in.wait()
+    t_in.wait()
     place(td, 1, p_of(x), lambda z: t_own[0, 0, z])
     place(tt, 1, q_of(y), lambda z: t_own[0, 0, z])
+
+    pattern_in.wait()
 
     def mask_step(z, carry):
         a_copy(z).wait()
@@ -189,10 +199,6 @@
     diagonal = lax.broadcasted_iota(jnp.int32, (blk, blk), 0) == lax.broadcasted_iota(
         jnp.int32, (blk, blk), 1
     )
-
-    def out_copy(which, z):
-        out = (pro_hbm, res_hbm)[which]
-        return pltpu.make_async_copy(obuf.at[which, z], out.at[0, 0, z], o_sem.at[which, z])
 
     def final_step(z, carry):
         centre = jnp.where(diagonal, a_v[z, 13].astype(F32), 0.0)
@@ -220,15 +226,12 @@
                         )
                         p, q = (h, v) if which == 0 else (v, h)
                         keep = hits(px)[p] * hits(qy)[q] * hits(r)[l]
-                        obuf[which, z, 4 * p + 2 * q + l] = (tile * keep - total).astype(BF)
-            out_copy(which, z).start()
+                        (pro, res)[which][0, 0, z, 4 * p + 2 * q + l] = (tile * keep - total).astype(BF)
         return carry
 
     lax.fori_loop(0, nz, final_step, 0)
 
     for z in range(nz):
-        out_copy(0, z).wait()
-        out_copy(1, z).wait()
         for d in range(4):
             @pl.when(has_dst[d])
             def _():
@@ -239,20 +242,34 @@
             t_copy(d).wait_send()
 
 
+def store_kernel(pro, res, pro_hbm, res_hbm, sem):
+    nz = pro.shape[2]
+    copies = [
+        pltpu.make_async_copy(src.at[0, 0, z], dst.at[0, 0, z], sem.at[i, z])
+        for i, (src, dst) in enumerate(((pro, pro_hbm), (res, res_hbm)))
+        for z in range(nz)
+    ]
+    for copy in copies:
+        copy.start()
+    for copy in copies:
+        copy.wait()
+
+
 def body(nx, ny, a_tiles, pattern, t_tiles, colour):
     nz, blk = a_tiles.shape[2], a_tiles.shape[-1]
+    colour = jnp.transpose(colour, (1, 2, 0))
     out = jax.ShapeDtypeStruct((1, 1, nz, SLOTS, blk, blk), BF)
-    return pl.pallas_call(
+    hbm = pl.BlockSpec(memory_space=pltpu.HBM)
+    vmem = pl.BlockSpec(memory_space=pltpu.VMEM)
+    pro, res = pl.pallas_call(
         functools.partial(kernel, nx, ny, nz, blk),
         out_shape=(out, out),
-        in_specs=[
-            pl.BlockSpec(memory_space=pltpu.SMEM),
-            pl.BlockSpec(memory_space=pltpu.SMEM),
-            pl.BlockSpec(memory_space=pl.ANY),
-            pl.BlockSpec(memory_space=pltpu.VMEM),
-        ],
-        out_specs=(pl.BlockSpec(memory_space=pl.ANY),) * 2,
+        in_specs=[hbm] * 4,
+        out_specs=(vmem, vmem),
         scratch_shapes=[
+            pltpu.SMEM(pattern.shape, jnp.int32),
+            pltpu.SMEM(colour.shape, jnp.int32),
+            pltpu.VMEM(t_tiles.shape, BF),
             pltpu.VMEM((nz, 27, blk, blk), BF),
             pltpu.VMEM((4, nz, blk, blk), BF),
             pltpu.VMEM((3, (nz + 2) * blk, 4 * blk), BF),
@@ -260,13 +277,12 @@
             pltpu.VMEM((4, nz, blk, 4 * blk), BF),
             pltpu.VMEM((4, nz, blk, 4 * blk), BF),
             pltpu.VMEM((2, nz, blk, 4 * blk), F32),
-            pltpu.VMEM((2, nz, SLOTS, blk, blk), BF),
+            pltpu.SemaphoreType.DMA((3,)),
             pltpu.SemaphoreType.DMA((nz,)),
             pltpu.SemaphoreType.DMA((4,)),
             pltpu.SemaphoreType.DMA((4,)),
             pltpu.SemaphoreType.DMA((4, nz)),
             pltpu.SemaphoreType.DMA((4, nz)),
-            pltpu.SemaphoreType.DMA((2, nz)),
         ],
         compiler_params=pltpu.CompilerParams(
             collective_id=0, has_side_effects=True, vmem_limit_bytes=48 * 1024 * 1024
@@ -274,7 +290,14 @@
         cost_estimate=pl.CostEstimate(
             flops=3_600_000_000, bytes_accessed=6_000_000, transcendentals=0
         ),
-    )(pattern, colour, a_tiles, t_tiles)
+    )(*(pltpu.with_memory_space_constraint(v, pltpu.HBM) for v in (pattern, colour, a_tiles, t_tiles)))
+    return pl.pallas_call(
+        store_kernel,
+        out_shape=(out, out),
+        in_specs=[vmem, vmem],
+        out_specs=(hbm, hbm),
+        scratch_shapes=[pltpu.SemaphoreType.DMA((2, nz))],
+    )(pro, res)
 
 
 def solution(mesh):

time: 32.4 us -> 29.6 us (0.914)
  local copies, waits for them, and re-layouts: 6.32 us -> 1.98 us
  Pallas kernels: 25.2 us -> 26.8 us
    unnamed x9 -> x4, local copies, waits for them, and re-layouts: 6.32 us -> 1.98 us
    pallas_call x0 -> x1, Pallas kernels: none -> 2.91 us  [body(): pl.pallas_call(store_kernel, out_shape=(out, out), in_specs=[vmem, vmem],...]
    pallas_call x1, Pallas kernels: 25.2 us -> 23.9 us  [body(): pl.pallas_call(functools.partial(kernel, nx, ny, nz, blk), out_shape=(out...]
where the time goes in v1:
time: 29.6 us; the launch traced here: 29.5 us
  Pallas kernels  26.8 us (91%)
  local copies, waits for them, and re-layouts  1.98 us (7%)
  between operations  0.65 us (2%)
    pallas_call x1, Pallas kernels, body(): pl.pallas_call(functools.partial(kernel, nx, ny, nz, blk), out_shape=(out...  23.9 us
    pallas_call x1, Pallas kernels, body(): pl.pallas_call(store_kernel, out_shape=(out, out), in_specs=[vmem, vmem],...  2.91 us
    unnamed x4, local copies, waits for them, and re-layouts  1.98 us

profile of v1, /device:TPU:0, one launch (start us, length us, event | category | flops | bytes accessed | tf_op | source)
XLA Modules:
  0.0 29.5 jit_solution(1213285153597273341)
XLA Ops:
  0.6 23.9 %shard_map.59 = (bf16[1,1,4,8,128,128]{5,4,3,2,1,0:T(8,128)(2,1)S(1)}, bf16[1,1,4,8,128,128]{5,4,3,2,1,0:T(8,128)(2,1)S(1)}) custom-call(s32[1,1,4,27]{3,2,1,0:T(4,128)} %pattern_hbm.1, s32[4,4,8]{2,1,0:T(4,128)} %bitcast.1, bf16[1,1,4,27,128,128]{5,4,3,2,1,0:T(8,128)(2,1)} %a_hbm.1, bf16[1,1,4,128,128]{4,3,2,1,0:T(8,128)(2,1)} %t_hbm.1), custom_call_target="tpu_custom_call" | custom-call | flops 3600000000 | bytes 6000000 | tf_op jit(solution)/shard_map/pallas_call | solution.py:264
  24.6 0.0 copy-start
  24.6 1.0 %copy-done = bf16[1,1,4,8,128,128]{5,4,3,2,1,0:T(8,128)(2,1)} copy-done((bf16[1,1,4,8,128,128]{5,4,3,2,1,0:T(8,128)(2,1)}, bf16[1,1,4,8,128,128]{5,4,3,2,1,0:T(8,128)(2,1)S(1)}, u32[]{:S(2)}) %copy-start) | copy-done | bytes 1048600
  25.5 0.0 copy-start.1
  25.5 1.0 %copy-done.1 = bf16[1,1,4,8,128,128]{5,4,3,2,1,0:T(8,128)(2,1)} copy-done((bf16[1,1,4,8,128,128]{5,4,3,2,1,0:T(8,128)(2,1)}, bf16[1,1,4,8,128,128]{5,4,3,2,1,0:T(8,128)(2,1)S(1)}, u32[]{:S(2)}) %copy-start.1) | copy-done | bytes 1048600
  26.5 2.9 %shard_map.60 = (bf16[1,1,4,8,128,128]{5,4,3,2,1,0:T(8,128)(2,1)}, bf16[1,1,4,8,128,128]{5,4,3,2,1,0:T(8,128)(2,1)}) custom-call(bf16[1,1,4,8,128,128]{5,4,3,2,1,0:T(8,128)(2,1)} %copy-done, bf16[1,1,4,8,128,128]{5,4,3,2,1,0:T(8,128)(2,1)} %copy-done.1), custom_call_target="tpu_custom_call" | custom-call | tf_op jit(solution)/shard_map/pallas_call | solution.py:294
Async XLA Ops:
  24.6 1.0 %copy-start = (bf16[1,1,4,8,128,128]{5,4,3,2,1,0:T(8,128)(2,1)}, bf16[1,1,4,8,128,128]{5,4,3,2,1,0:T(8,128)(2,1)S(1)}, u32[]{:S(2)}) copy-start(bf16[1,1,4,8,128,128]{5,4,3,2,1,0:T(8,128)(2,1)S(1)} %get-tuple-element.4.pro) | copy-start | bytes 3145732
  25.5 1.0 %copy-start.1 = (bf16[1,1,4,8,128,128]{5,4,3,2,1,0:T(8,128)(2,1)}, bf16[1,1,4,8,128,128]{5,4,3,2,1,0:T(8,128)(2,1)S(1)}, u32[]{:S(2)}) copy-start(bf16[1,1,4,8,128,128]{5,4,3,2,1,0:T(8,128)(2,1)S(1)} %get-tuple-element.5.res) | copy-start | bytes 3145732

commit v2 on v1

--- a/solution.py
+++ b/solution.py
@@ -285,7 +285,7 @@
             pltpu.SemaphoreType.DMA((4, nz)),
         ],
         compiler_params=pltpu.CompilerParams(
-            collective_id=0, has_side_effects=True, vmem_limit_bytes=48 * 1024 * 1024
+            collective_id=0, has_side_effects=True, vmem_limit_bytes=28 * 1024 * 1024
         ),
         cost_estimate=pl.CostEstimate(
             flops=3_600_000_000, bytes_accessed=6_000_000, transcendentals=0
@@ -296,7 +296,7 @@
         out_shape=(out, out),
         in_specs=[vmem, vmem],
         out_specs=(hbm, hbm),
-        scratch_shapes=[pltpu.SemaphoreType.DMA((2, nz))],
+        scratch_shapes=[pltpu.SemaphoreType.DMA((2, nz))],compiler_params=pltpu.CompilerParams(vmem_limit_bytes=2*1024*1024),
     )(pro, res)
 
 

time: 29.6 us -> 26.1 us (0.88)
  local copies, waits for them, and re-layouts: 1.98 us -> 0 us
  Pallas kernels: 26.8 us -> 25.3 us
    unnamed x4 -> x0, local copies, waits for them, and re-layouts: 1.98 us -> none
    pallas_call x1, Pallas kernels: 2.91 us -> 1.38 us  [body(): pl.pallas_call(store_kernel, out_shape=(out, out), in_specs=[vmem, vmem],...]
where the time goes in v2:
time: 26.1 us; the launch traced here: 25.9 us
  Pallas kernels  25.3 us (97%)
  between operations  0.64 us (2%)
    pallas_call x1, Pallas kernels, body(): pl.pallas_call(functools.partial(kernel, nx, ny, nz, blk), out_shape=(out...  23.9 us
    pallas_call x1, Pallas kernels, body(): pl.pallas_call(store_kernel, out_shape=(out, out), in_specs=[vmem, vmem],...  1.38 us

profile of v2, /device:TPU:0, one launch (start us, length us, event | category | flops | bytes accessed | tf_op | source)
XLA Modules:
  0.0 25.9 jit_solution(16342654691100861922)
XLA Ops:
  0.6 23.9 %shard_map.59 = (bf16[1,1,4,8,128,128]{5,4,3,2,1,0:T(8,128)(2,1)S(1)}, bf16[1,1,4,8,128,128]{5,4,3,2,1,0:T(8,128)(2,1)S(1)}) custom-call(s32[1,1,4,27]{3,2,1,0:T(4,128)} %pattern_hbm.1, s32[4,4,8]{2,1,0:T(4,128)} %bitcast.1, bf16[1,1,4,27,128,128]{5,4,3,2,1,0:T(8,128)(2,1)} %a_hbm.1, bf16[1,1,4,128,128]{4,3,2,1,0:T(8,128)(2,1)} %t_hbm.1), custom_call_target="tpu_custom_call" | custom-call | flops 3600000000 | bytes 6000000 | tf_op jit(solution)/shard_map/pallas_call | solution.py:264
  24.6 1.4 %shard_map.60 = (bf16[1,1,4,8,128,128]{5,4,3,2,1,0:T(8,128)(2,1)}, bf16[1,1,4,8,128,128]{5,4,3,2,1,0:T(8,128)(2,1)}) custom-call(bf16[1,1,4,8,128,128]{5,4,3,2,1,0:T(8,128)(2,1)S(1)} %get-tuple-element.4.pro, bf16[1,1,4,8,128,128]{5,4,3,2,1,0:T(8,128)(2,1)S(1)} %get-tuple-element.5.res), custom_call_target="tpu_custom_call" | custom-call | tf_op jit(solution)/shard_map/pallas_call | solution.py:294

commit v3 on v2

--- a/solution.py
+++ b/solution.py
@@ -16,14 +16,18 @@
 def kernel(
     nx, ny, nz, blk,
     pattern_hbm, colour_hbm, a_hbm, t_hbm, pro, res,
-    pattern, colour, t_own, a_v, th, td, tt, sbuf, rbuf, own,
-    in_sem, a_sem, th_send, th_recv, p_send, p_recv,
+    pattern, colour, t_own, a_v, th, td, tt, sbuf, rbuf, own, hop,
+    in_sem, a_sem, th_send, th_recv, p_send, p_recv, h_send, h_recv, f_send,
 ):
     x = lax.axis_index("row")
     y = lax.axis_index("col")
     has_dst = (x > 0, x < nx - 1, y > 0, y < ny - 1)
     has_src = (x < nx - 1, x > 0, y < ny - 1, y > 0)
     peers = ((x - 1, y), (x + 1, y), (x, y - 1), (x, y + 1))
+
+    hops = nz // 2 if nx == 8 else 0
+    ends = ((4, 3), (3, 4))
+    via = (0, nx - 1)
 
     def a_copy(z):
         return pltpu.make_async_copy(a_hbm.at[0, 0, z], a_v.at[z], a_sem.at[z])
@@ -45,6 +49,17 @@
                 barrier, inc=1, device_id=peers[d], device_id_type=pl.DeviceIdType.MESH
             )
     count = sum(h.astype(jnp.int32) for h in has_dst)
+    if hops:
+        for mine, others in ((ends[0], via), (via, ends[0])):
+            here = (x == mine[0]) | (x == mine[1])
+            @pl.when(here)
+            def _():
+                for other in others:
+                    pl.semaphore_signal(
+                        barrier, inc=1, device_id=(other, y),
+                        device_id_type=pl.DeviceIdType.MESH,
+                    )
+            count = count + 2 * here.astype(jnp.int32)
     pl.semaphore_wait(barrier, count)
 
     def t_copy(d):
@@ -60,6 +75,33 @@
             send_sem=p_send.at[d, z], recv_sem=p_recv.at[d, z],
             device_id=peers[d], device_id_type=pl.DeviceIdType.MESH,
         )
+
+    def hop_copy(d, z):
+        return pltpu.make_async_remote_copy(
+            src_ref=sbuf.at[d, z], dst_ref=hop.at[z],
+            send_sem=h_send.at[z], recv_sem=h_recv.at[z],
+            device_id=(via[d], y), device_id_type=pl.DeviceIdType.MESH,
+        )
+
+    def forward(d, z):
+        return pltpu.make_async_remote_copy(
+            src_ref=hop.at[z], dst_ref=rbuf.at[d, z],
+            send_sem=f_send.at[z], recv_sem=p_recv.at[d, z],
+            device_id=(ends[d][1], y), device_id_type=pl.DeviceIdType.MESH,
+        )
+
+    def send(d, z, do):
+        by_hop = False
+        if hops and d < 2:
+            by_hop = (x == ends[d][0]) & (z < hops)
+
+            @pl.when(by_hop)
+            def _():
+                do(hop_copy(d, jnp.minimum(z, hops - 1)))
+
+        @pl.when(jnp.logical_and(has_dst[d], jnp.logical_not(by_hop)))
+        def _():
+            do(p_copy(d, z))
 
     for d in (2, 3, 0, 1):
         @pl.when(has_dst[d])
@@ -123,16 +165,11 @@
 
     lax.fori_loop(0, nz, mask_step, 0)
 
-    for d, dst, which, high in (
-        (0, td, 2, p_of(x + 1)),
-        (1, td, 0, p_of(x - 1)),
-        (2, tt, 2, q_of(y + 1)),
-        (3, tt, 0, q_of(y - 1)),
-    ):
+    def take(d, dst, which, high):
         @pl.when(has_src[d])
         def _():
             t_copy(d).wait_recv()
-        place(dst, which, high, lambda z, d=d: th[d, z])
+        place(dst, which, high, lambda z: th[d, z])
 
     def direct(z, y_steps):
         rows = pl.ds(pl.multiple_of(z * blk, blk), 3 * blk)
@@ -169,24 +206,23 @@
             left, right, (((0,), (0,)), ((), ())), preferred_element_type=F32
         )
 
-    def edge_step(z, carry):
-        part = direct(z, (1, -1)).astype(BF)
-        sbuf[2, z] = part[:blk]
-        sbuf[3, z] = part[blk:]
-        for d in (2, 3):
-            @pl.when(has_dst[d])
-            def _():
-                p_copy(d, z).start()
-        part = transposed(z, (-1, 1)).astype(BF)
-        sbuf[0, z] = part[:blk]
-        sbuf[1, z] = part[blk:]
-        for d in (0, 1):
-            @pl.when(has_dst[d])
-            def _():
-                p_copy(d, z).start()
-        return carry
-
-    lax.fori_loop(0, nz, edge_step, 0)
+    def edge(product, steps, first):
+        def step(z, carry):
+            part = product(z, steps).astype(BF)
+            for k in range(2):
+                d = first + k
+                sbuf[d, z] = part[k * blk : (k + 1) * blk]
+                send(d, z, lambda copy: copy.start())
+            return carry
+
+        lax.fori_loop(0, nz, step, 0)
+
+    take(0, td, 2, p_of(x + 1))
+    take(1, td, 0, p_of(x - 1))
+    edge(direct, (1, -1), 2)
+    take(2, tt, 2, q_of(y + 1))
+    take(3, tt, 0, q_of(y - 1))
+    edge(transposed, (-1, 1), 0)
 
     def own_step(z, carry):
         own[0, z] = direct(z, (0,))
@@ -194,6 +230,14 @@
         return carry
 
     lax.fori_loop(0, nz, own_step, 0)
+
+    for d in range(2):
+        if hops:
+            @pl.when(x == via[d])
+            def _():
+                for z in range(hops):
+                    hop_copy(d, z).wait_recv()
+                    forward(d, z).start()
 
     px, qy = p_of(x), q_of(y)
     diagonal = lax.broadcasted_iota(jnp.int32, (blk, blk), 0) == lax.broadcasted_iota(
@@ -233,9 +277,13 @@
 
     for z in range(nz):
         for d in range(4):
-            @pl.when(has_dst[d])
+            send(d, z, lambda copy: copy.wait_send())
+    for d in range(2):
+        if hops:
+            @pl.when(x == via[d])
             def _():
-                p_copy(d, z).wait_send()
+                for z in range(hops):
+                    forward(d, z).wait_send()
     for d in range(4):
         @pl.when(has_dst[d])
         def _():
@@ -277,12 +325,16 @@
             pltpu.VMEM((4, nz, blk, 4 * blk), BF),
             pltpu.VMEM((4, nz, blk, 4 * blk), BF),
             pltpu.VMEM((2, nz, blk, 4 * blk), F32),
+            pltpu.VMEM((nz // 2, blk, 4 * blk), BF),
             pltpu.SemaphoreType.DMA((3,)),
             pltpu.SemaphoreType.DMA((nz,)),
             pltpu.SemaphoreType.DMA((4,)),
             pltpu.SemaphoreType.DMA((4,)),
             pltpu.SemaphoreType.DMA((4, nz)),
             pltpu.SemaphoreType.DMA((4, nz)),
+            pltpu.SemaphoreType.DMA((nz // 2,)),
+            pltpu.SemaphoreType.DMA((nz // 2,)),
+            pltpu.SemaphoreType.DMA((nz // 2,)),
         ],
         compiler_params=pltpu.CompilerParams(
             collective_id=0, has_side_effects=True, vmem_limit_bytes=28 * 1024 * 1024

time: 26.1 us -> 24.4 us (0.935)
  the two profiles are of different devices: /device:TPU:0 before, /device:TPU:28 now
where the time goes in v3:
time: 24.4 us; the launch traced here: 24.3 us
  Pallas kernels  23.6 us (97%)
  between operations  0.64 us (3%)
    pallas_call x1, Pallas kernels, body(): pl.pallas_call(functools.partial(kernel, nx, ny, nz, blk), out_shape=(out...  22.3 us
    pallas_call x1, Pallas kernels, body(): pl.pallas_call(store_kernel, out_shape=(out, out), in_specs=[vmem, vmem],...  1.38 us

profile of v3, /device:TPU:28, one launch (start us, length us, event | category | flops | bytes accessed | tf_op | source)
XLA Modules:
  0.0 24.3 jit_solution(3189683989149555027)
XLA Ops:
  0.6 22.3 %shard_map.59 = (bf16[1,1,4,8,128,128]{5,4,3,2,1,0:T(8,128)(2,1)S(1)}, bf16[1,1,4,8,128,128]{5,4,3,2,1,0:T(8,128)(2,1)S(1)}) custom-call(s32[1,1,4,27]{3,2,1,0:T(4,128)} %pattern_hbm.1, s32[4,4,8]{2,1,0:T(4,128)} %bitcast.1, bf16[1,1,4,27,128,128]{5,4,3,2,1,0:T(8,128)(2,1)} %a_hbm.1, bf16[1,1,4,128,128]{4,3,2,1,0:T(8,128)(2,1)} %t_hbm.1), custom_call_target="tpu_custom_call" | custom-call | flops 3600000000 | bytes 6000000 | tf_op jit(solution)/shard_map/pallas_call | solution.py:312
  22.9 1.4 %shard_map.60 = (bf16[1,1,4,8,128,128]{5,4,3,2,1,0:T(8,128)(2,1)}, bf16[1,1,4,8,128,128]{5,4,3,2,1,0:T(8,128)(2,1)}) custom-call(bf16[1,1,4,8,128,128]{5,4,3,2,1,0:T(8,128)(2,1)S(1)} %get-tuple-element.4.pro, bf16[1,1,4,8,128,128]{5,4,3,2,1,0:T(8,128)(2,1)S(1)} %get-tuple-element.5.res), custom_call_target="tpu_custom_call" | custom-call | tf_op jit(solution)/shard_map/pallas_call | solution.py:346

commit v4 on v3

--- a/solution.py
+++ b/solution.py
@@ -206,7 +206,7 @@
             left, right, (((0,), (0,)), ((), ())), preferred_element_type=F32
         )
 
-    def edge(product, steps, first):
+    def edge(product, steps, first, low, high):
         def step(z, carry):
             part = product(z, steps).astype(BF)
             for k in range(2):
@@ -215,14 +215,16 @@
                 send(d, z, lambda copy: copy.start())
             return carry
 
-        lax.fori_loop(0, nz, step, 0)
+        lax.fori_loop(low, high, step, 0)
 
     take(0, td, 2, p_of(x + 1))
     take(1, td, 0, p_of(x - 1))
-    edge(direct, (1, -1), 2)
+    edge(direct, (1, -1), 2, 0, nz // 2)
     take(2, tt, 2, q_of(y + 1))
     take(3, tt, 0, q_of(y - 1))
-    edge(transposed, (-1, 1), 0)
+    edge(transposed, (-1, 1), 0, 0, nz // 2)
+    edge(direct, (1, -1), 2, nz // 2, nz)
+    edge(transposed, (-1, 1), 0, nz // 2, nz)
 
     def own_step(z, carry):
         own[0, z] = direct(z, (0,))

time: 24.4 us -> 23.7 us (0.971)
  the two profiles are of different devices: /device:TPU:28 before, /device:TPU:12 now
where the time goes in v4:
time: 23.7 us; the launch traced here: 23.6 us
  Pallas kernels  22.9 us (97%)
  between operations  0.64 us (3%)
    pallas_call x1, Pallas kernels, body(): pl.pallas_call(functools.partial(kernel, nx, ny, nz, blk), out_shape=(out...  21.5 us
    pallas_call x1, Pallas kernels, body(): pl.pallas_call(store_kernel, out_shape=(out, out), in_specs=[vmem, vmem],...  1.38 us

profile of v4, /device:TPU:12, one launch (start us, length us, event | category | flops | bytes accessed | tf_op | source)
XLA Modules:
  0.0 23.6 jit_solution(16331581379348111643)
XLA Ops:
  0.6 21.5 %shard_map.59 = (bf16[1,1,4,8,128,128]{5,4,3,2,1,0:T(8,128)(2,1)S(1)}, bf16[1,1,4,8,128,128]{5,4,3,2,1,0:T(8,128)(2,1)S(1)}) custom-call(s32[1,1,4,27]{3,2,1,0:T(4,128)} %pattern_hbm.1, s32[4,4,8]{2,1,0:T(4,128)} %bitcast.1, bf16[1,1,4,27,128,128]{5,4,3,2,1,0:T(8,128)(2,1)} %a_hbm.1, bf16[1,1,4,128,128]{4,3,2,1,0:T(8,128)(2,1)} %t_hbm.1), custom_call_target="tpu_custom_call" | custom-call | flops 3600000000 | bytes 6000000 | tf_op jit(solution)/shard_map/pallas_call | solution.py:314
  22.2 1.4 %shard_map.60 = (bf16[1,1,4,8,128,128]{5,4,3,2,1,0:T(8,128)(2,1)}, bf16[1,1,4,8,128,128]{5,4,3,2,1,0:T(8,128)(2,1)}) custom-call(bf16[1,1,4,8,128,128]{5,4,3,2,1,0:T(8,128)(2,1)S(1)} %get-tuple-element.4.pro, bf16[1,1,4,8,128,128]{5,4,3,2,1,0:T(8,128)(2,1)S(1)} %get-tuple-element.5.res), custom_call_target="tpu_custom_call" | custom-call | tf_op jit(solution)/shard_map/pallas_call | solution.py:348

commit v5 on v4

--- a/solution.py
+++ b/solution.py
@@ -103,7 +103,7 @@
         def _():
             do(p_copy(d, z))
 
-    for d in (2, 3, 0, 1):
+    for d in (0, 1, 2, 3):
         @pl.when(has_dst[d])
         def _():
             t_copy(d).start()

time: 23.7 us -> 23.6 us (level)
  no operation moved by 1% of the time
where the time goes in v5:
time: 23.6 us; the launch traced here: 23.5 us
  Pallas kernels  22.8 us (97%)
  between operations  0.64 us (3%)
    pallas_call x1, Pallas kernels, body(): pl.pallas_call(functools.partial(kernel, nx, ny, nz, blk), out_shape=(out...  21.5 us
    pallas_call x1, Pallas kernels, body(): pl.pallas_call(store_kernel, out_shape=(out, out), in_specs=[vmem, vmem],...  1.38 us

profile of v5, /device:TPU:12, one launch (start us, length us, event | category | flops | bytes accessed | tf_op | source)
XLA Modules:
  0.0 23.5 jit_solution(16005747005627915213)
XLA Ops:
  0.6 21.5 %shard_map.59 = (bf16[1,1,4,8,128,128]{5,4,3,2,1,0:T(8,128)(2,1)S(1)}, bf16[1,1,4,8,128,128]{5,4,3,2,1,0:T(8,128)(2,1)S(1)}) custom-call(s32[1,1,4,27]{3,2,1,0:T(4,128)} %pattern_hbm.1, s32[4,4,8]{2,1,0:T(4,128)} %bitcast.1, bf16[1,1,4,27,128,128]{5,4,3,2,1,0:T(8,128)(2,1)} %a_hbm.1, bf16[1,1,4,128,128]{4,3,2,1,0:T(8,128)(2,1)} %t_hbm.1), custom_call_target="tpu_custom_call" | custom-call | flops 3600000000 | bytes 6000000 | tf_op jit(solution)/shard_map/pallas_call | solution.py:314
  22.1 1.4 %shard_map.60 = (bf16[1,1,4,8,128,128]{5,4,3,2,1,0:T(8,128)(2,1)}, bf16[1,1,4,8,128,128]{5,4,3,2,1,0:T(8,128)(2,1)}) custom-call(bf16[1,1,4,8,128,128]{5,4,3,2,1,0:T(8,128)(2,1)S(1)} %get-tuple-element.4.pro, bf16[1,1,4,8,128,128]{5,4,3,2,1,0:T(8,128)(2,1)S(1)} %get-tuple-element.5.res), custom_call_target="tpu_custom_call" | custom-call | tf_op jit(solution)/shard_map/pallas_call | solution.py:348
